TPU v7x, 128 devices: a whole 4x4x4 slice. The times are simulated.
128 devices in a mesh: grp: 2 (over core), dp: 4 (over z), ep: 16 (over x, y).
Axes of the slice: x: 4, y: 4, z: 4, core: 2. Of those that a mesh axis runs over, the one named last changes fastest.
Arguments:
- tokens: bfloat16 [2048, 2048], P(('grp', 'dp', 'ep')), may hold values from -6 to 6
- think_gain: float32 [2048], replicated, may hold values from 0.1 to 1.9
- think_routes: int32 [2048, 8], P(('grp', 'dp', 'ep')), may hold values from 0 to 127, all different within a row; in each aligned block of 16 rows (0 to 15, 16 to 31, ...) at most 2 rows name the same one
- think_weights: float32 [2048, 8], P(('grp', 'dp', 'ep')), may hold values from 0.1 to 1
- think_keep: int32 [2048, 8], P(('grp', 'dp', 'ep')), may hold values 0 or 1
- think_gate_up: bfloat16 [128, 2048, 1536], P(('grp', 'dp', 'ep')), may hold values from -0.125 to 0.125
- think_down: bfloat16 [128, 768, 2048], P(('grp', 'dp', 'ep')), may hold values from -0.21875 to 0.21875
- talk_proj: bfloat16 [2048, 1024], replicated, may hold values from -0.125 to 0.125
- codec_table: bfloat16 [3072, 1024], replicated, may hold values from -6 to 6
- codec_ids: int32 [2048], P(('grp', 'dp', 'ep')), may hold values from 0 to 3071
- talk_gain: float32 [1024], replicated, may hold values from 0.1 to 1.9
- talk_routes: int32 [2048, 8], P(('grp', 'dp', 'ep')), may hold values from 0 to 127, all different within a row; in each aligned block of 16 rows (0 to 15, 16 to 31, ...) at most 2 rows name the same one
- talk_weights: float32 [2048, 8], P(('grp', 'dp', 'ep')), may hold values from 0.1 to 1
- talk_keep: int32 [2048, 8], P(('grp', 'dp', 'ep')), may hold values 0 or 1
- talk_gate_up: bfloat16 [128, 1024, 768], P(('grp', 'dp', 'ep')), may hold values from -0.1875 to 0.1875
- talk_down: bfloat16 [128, 384, 1024], P(('grp', 'dp', 'ep')), may hold values from -0.3125 to 0.3125
Outputs:
- think_out: bfloat16 [2048, 2048], P(('grp', 'dp', 'ep'))
- talk_out: bfloat16 [2048, 1024], P(('grp', 'dp', 'ep'))
Inputs may be any that keep to these rules, and one draw needn't show every extreme that they name: `think_routes`: within the rows of one device, no expert is named more than 2 times, a bound that some block reaches. `talk_routes`: within the rows of one device, no expert is named more than 2 times, a bound that some block reaches.
All inputs are finite; a program needn't handle non-finite values. No bound on the sum of `think_keep` or of `talk_keep` on one device may be relied on, other than what follows from the above.
Results may differ from a plain program's by a relative error of at most 0.006.
Values may be sent and summed in bfloat16 or wider, within the bound.
A program may use at most 64 MiB of HBM per device.

v0:
```python
import jax
import jax.numpy as jnp
from jax import lax
from jax.sharding import PartitionSpec as P


def normed(inputs, norm_gain):
    values = inputs.astype(jnp.float32)
    inverse_rms = lax.rsqrt(jnp.mean(values * values, axis=-1, keepdims=True) + 1e-06)
    return (values * inverse_rms * norm_gain).astype(jnp.bfloat16)


def fill_bins(normed_rows, routes, expert_count, capacity):
    flat_routes = routes.reshape(-1)
    matches = (flat_routes[:, None] == jnp.arange(expert_count, dtype=jnp.int32)[None, :]).astype(
        jnp.int32
    )
    earlier = jnp.cumsum(matches, axis=0) - matches
    slot_index = jnp.sum(earlier * matches, axis=1)
    positions = flat_routes * capacity + slot_index
    repeated = jnp.repeat(normed_rows, routes.shape[1], axis=0)
    row_width = normed_rows.shape[1]
    bin_rows = (
        jnp.zeros((expert_count * capacity, row_width), jnp.bfloat16).at[positions].set(repeated)
    )
    return (bin_rows.reshape(expert_count, capacity, row_width), positions)


def run_experts(received, gate_up, down_proj):
    local_count = gate_up.shape[0]
    grouped = received.reshape(-1, local_count, received.shape[1], received.shape[2])
    joined = jnp.einsum("sekw,ewf->sekf", grouped, gate_up, preferred_element_type=jnp.float32)
    split_at = gate_up.shape[2] // 2
    hidden_act = (jax.nn.silu(joined[..., :split_at]) * joined[..., split_at:]).astype(jnp.bfloat16)
    results = jnp.einsum(
        "sekf,efw->sekw", hidden_act, down_proj, preferred_element_type=jnp.float32
    )
    return results.astype(jnp.bfloat16).reshape(received.shape)


def mix_back(residual, returned, weights, keep):
    shares = weights * keep.astype(jnp.float32) / jnp.sum(weights, axis=1, keepdims=True)
    return residual.astype(jnp.float32) + jnp.sum(
        shares[:, :, None] * returned.astype(jnp.float32), axis=1
    )


def think_layer(bin_rows, gate_up, down_proj):
    return lax.all_to_all(
        run_experts(
            lax.all_to_all(bin_rows, ("grp", "dp", "ep"), split_axis=0, concat_axis=0, tiled=True),
            gate_up,
            down_proj,
        ),
        ("grp", "dp", "ep"),
        split_axis=0,
        concat_axis=0,
        tiled=True,
    )


def talk_layer(bin_rows, gate_up, down_proj):
    return lax.all_to_all(
        run_experts(
            lax.all_to_all(bin_rows, ("grp", "dp", "ep"), split_axis=0, concat_axis=0, tiled=True),
            gate_up,
            down_proj,
        ),
        ("grp", "dp", "ep"),
        split_axis=0,
        concat_axis=0,
        tiled=True,
    )


def shards(
    tokens,
    think_gain,
    think_routes,
    think_weights,
    think_keep,
    think_gate_up,
    think_down,
    talk_proj,
    codec_table,
    codec_ids,
    talk_gain,
    talk_routes,
    talk_weights,
    talk_keep,
    talk_gate_up,
    talk_down,
):
    device_count = lax.axis_size(("grp", "dp", "ep"))
    expert_count = think_gate_up.shape[0] * device_count
    top_count = think_routes.shape[1]
    row_count = tokens.shape[0]
    capacity = 2 * row_count * top_count // expert_count
    think_norm = normed(tokens, think_gain)
    think_bins, think_positions = fill_bins(think_norm, think_routes, expert_count, capacity)
    think_return = think_layer(think_bins, think_gate_up, think_down)
    think_expert = think_return.reshape(-1, tokens.shape[1])[think_positions].reshape(
        row_count, top_count, tokens.shape[1]
    )
    think_out = mix_back(tokens, think_expert, think_weights, think_keep).astype(jnp.bfloat16)
    talk_input = jnp.dot(think_out, talk_proj, preferred_element_type=jnp.float32) + codec_table[
        codec_ids
    ].astype(jnp.float32)
    talk_norm = normed(talk_input, talk_gain)
    talk_width = talk_input.shape[1]
    talk_bins, talk_positions = fill_bins(talk_norm, talk_routes, expert_count, capacity)
    talk_return = talk_layer(talk_bins, talk_gate_up, talk_down)
    talk_expert = talk_return.reshape(-1, talk_width)[talk_positions].reshape(
        row_count, top_count, talk_width
    )
    talk_out = mix_back(talk_input, talk_expert, talk_weights, talk_keep).astype(jnp.bfloat16)
    return (think_out, talk_out)


def solution(mesh):
    placed = (
        P(("grp", "dp", "ep"), None),
        P(),
        P(("grp", "dp", "ep"), None),
        P(("grp", "dp", "ep"), None),
        P(("grp", "dp", "ep"), None),
        P(("grp", "dp", "ep"), None, None),
        P(("grp", "dp", "ep"), None, None),
        P(),
        P(),
        P(("grp", "dp", "ep")),
        P(),
        P(("grp", "dp", "ep"), None),
        P(("grp", "dp", "ep"), None),
        P(("grp", "dp", "ep"), None),
        P(("grp", "dp", "ep"), None, None),
        P(("grp", "dp", "ep"), None, None),
    )
    return jax.shard_map(
        shards,
        mesh=mesh,
        in_specs=placed,
        out_specs=(P(("grp", "dp", "ep"), None), P(("grp", "dp", "ep"), None)),
        check_vma=False,
    )
```

profile of v0, /device:TPU:1, one launch (start us, length us, event | category | flops | bytes accessed | tf_op | source)
XLA Modules:
  0.0 131.3 jit_solution(480579109780979002)
XLA Ops:
  0.6 0.0 copy-start
  0.7 0.9 copy.36
  1.6 0.7 broadcast_multiply_fusion.1
  2.3 0.1 eq.30
  2.4 0.1 fusion.39
  2.5 0.2 reduce_window_sum.17
  2.7 0.2 select_reduce_fusion.1
  2.8 0.1 copy.35
  2.9 0.1 mul.109
  3.0 1.0 fusion.33
  4.0 0.9 fusion.35
  4.9 2.5 %scatter_custom_fusion = bf16[256,2048]{1,0:T(8,128)(2,1)} fusion(s32[128]{0:T(128)S(1)} %fusion.40, bf16[]{:T(256)} %constant.11.clone.1, bf16[16,2048]{1,0:T(8,128)(2,1)S(1)} %fusion.35), kind=kCustom, calls=%fused_computation.24 | custom fusion | bytes 1114114 | tf_op jit(solution)/shard_map/scatter | solution.py:24
  7.4 2.5 %reshape.143 = bf16[128,2,2048]{2,1,0:T(2,128)(2,1)} reshape(bf16[256,2048]{1,0:T(8,128)(2,1)} %scatter_custom_fusion) | data formatting | bytes 2097152 | tf_op jit(solution)/shard_map/reshape | solution.py:26
  10.0 12.0 %all-to-all-start = ((bf16[128,2,2048]{2,1,0:T(2,128)(2,1)}), bf16[128,2,2048]{2,1,0:T(2,128)(2,1)}, u32[]{:S(2)}, u32[]{:S(2)}) async-start(bf16[128,2,2048]{2,1,0:T(2,128)(2,1)} %reshape.143), calls=%async_computation | async-start | bytes 2097152 | tf_op jit(solution)/shard_map/all_to_all | solution.py:51
  22.0 0.1 copy.41
  22.0 0.1 eq.34
  22.2 0.1 fusion.38
  22.2 17.3 %all-to-all-done = bf16[128,2,2048]{2,1,0:T(2,128)(2,1)} async-done(((bf16[128,2,2048]{2,1,0:T(2,128)(2,1)}), bf16[128,2,2048]{2,1,0:T(2,128)(2,1)}, u32[]{:S(2)}, u32[]{:S(2)}) %all-to-all-start) | async-done | bytes 1048608 | tf_op jit(solution)/shard_map/all_to_all | solution.py:51
  39.5 4.9 %fusion.4 = f32[128,1,2,1536]{3,0,2,1:T(8,128)S(1)} fusion(bf16[1,2048,1536]{2,1,0:T(8,128)(2,1)} %param.21, bf16[128,2,2048]{2,1,0:T(2,128)(2,1)} %all-to-all-done), kind=kOutput, calls=%fused_computation.9 | convolution fusion | flops 1610612736 | bytes 8912896 | tf_op jit(solution)/shard_map/sekw,ewf->sekf/dot_general | solution.py:32
  44.4 1.0 fusion.7
  45.5 2.1 %copy.38 = bf16[128,2,2048]{2,1,0:T(2,128)(2,1)} copy(bf16[128,2,2048]{2,0,1:T(8,128)(2,1)S(1)} %fusion.7) | data formatting | bytes 2097152 | tf_op jit(solution)/shard_map/convert_element_type | solution.py:38
  47.6 5.9 %all-to-all-start.1 = ((bf16[128,2,2048]{2,1,0:T(2,128)(2,1)}), bf16[128,2,2048]{2,1,0:T(2,128)(2,1)}, u32[]{:S(2)}, u32[]{:S(2)}) async-start(bf16[128,2,2048]{2,1,0:T(2,128)(2,1)} %copy.38), calls=%async_computation.1 | async-start | bytes 2097152 | tf_op jit(solution)/shard_map/all_to_all | solution.py:49
  53.6 0.1 copy.34
  53.6 0.2 reduce_window_sum.18
  53.8 0.1 copy.40
  53.9 0.1 mul.122
  54.0 4.2 %gather_fusion.1 = bf16[16,1024]{1,0:T(8,128)(2,1)S(1)} fusion(bf16[3072,1024]{1,0:T(8,128)(2,1)} %param.24, s32[1024]{0:T(1024)S(1)} %pad_clamp_fusion.1), kind=kCustom, calls=%fused_computation.1 | custom fusion | bytes 65600 | tf_op jit(solution)/shard_map/gather | solution.py:106
  58.2 0.2 select_reduce_fusion
  58.4 12.7 %all-to-all-done.1 = bf16[128,2,2048]{2,1,0:T(2,128)(2,1)} async-done(((bf16[128,2,2048]{2,1,0:T(2,128)(2,1)}), bf16[128,2,2048]{2,1,0:T(2,128)(2,1)}, u32[]{:S(2)}, u32[]{:S(2)}) %all-to-all-start.1) | async-done | bytes 1048608 | tf_op jit(solution)/shard_map/all_to_all | solution.py:49
  71.1 2.3 %reshape.147 = bf16[256,2048]{1,0:T(8,128)(2,1)} reshape(bf16[128,2,2048]{2,1,0:T(2,128)(2,1)} %all-to-all-done.1) | data formatting | bytes 2097152 | tf_op jit(solution)/shard_map/reshape | solution.py:102
  73.4 3.6 %gather_fusion = bf16[128,2048]{1,0:T(8,128)(2,1)} fusion(bf16[256,2048]{1,0:T(8,128)(2,1)} %reshape.147, s32[1024]{0:T(1024)S(1)} %pad_clamp_fusion.2), kind=kCustom, calls=%fused_computation | custom fusion | bytes 1049088 | tf_op jit(solution)/shard_map/gather | solution.py:102
  77.0 1.5 %fusion.15 = f32[16,2048]{1,0:T(8,128)S(1)} fusion(bf16[128,2048]{1,0:T(8,128)(2,1)} %gather_fusion, f32[16,8]{1,0:T(8,128)S(1)} %copy.34), kind=kLoop, calls=%fused_computation.17 | loop fusion | flops 753664 | bytes 655872 | tf_op jit(solution)/shard_map/reduce_sum | solution.py:43
  78.5 0.0 copy-start.2
  78.5 3.0 %multiply_reduce_fusion = (f32[16]{0:T(128)S(1)}, f32[16,1024]{1,0:T(8,128)S(1)}) fusion(bf16[16,1024]{1,0:T(8,128)(2,1)S(1)} %gather_fusion.1, bf16[16,2048]{1,0:T(8,128)(2,1)S(1)} %fusion.36, bf16[2048,1024]{1,0:T(8,128)(2,1)} %param.23), kind=kOutput, calls=%fused_computation.46 | convolution fusion | flops 67174384 | bytes 4358208 | tf_op jit(solution)/shard_map/dot_general | solution.py:106
  81.5 0.1 multiply_convert_fusion
  81.6 2.0 %scatter_custom_fusion.1 = bf16[256,1024]{1,0:T(8,128)(2,1)} fusion(s32[128]{0:T(128)S(1)} %fusion.41, bf16[]{:T(256)} %constant.11.clone.1, bf16[16,1024]{1,0:T(8,128)(2,1)S(1)} %multiply_convert_fusion), kind=kCustom, calls=%fused_computation.31 | custom fusion | bytes 557058 | tf_op jit(solution)/shard_map/scatter | solution.py:24
  83.6 2.0 %reshape.149 = bf16[128,2,1024]{2,1,0:T(2,128)(2,1)} reshape(bf16[256,1024]{1,0:T(8,128)(2,1)} %scatter_custom_fusion.1) | data formatting | bytes 1048576 | tf_op jit(solution)/shard_map/reshape | solution.py:26
  85.6 18.5 %all_to_all.20 = bf16[128,2,1024]{2,1,0:T(2,128)(2,1)S(1)} all-to-all(bf16[128,2,1024]{2,1,0:T(2,128)(2,1)} %reshape.149), channel_id=1, replica_groups=mesh['grp'=2,'dp'=4,'ep'=16] {'grp','dp','ep'}, dimensions={0} | all-to-all | bytes 1048576 | tf_op jit(solution)/shard_map/all_to_all | solution.py:65
  104.2 2.0 %fusion.12 = f32[128,1,2,768]{3,0,2,1:T(8,128)S(1)} fusion(bf16[1,1024,768]{2,1,0:T(8,128)(2,1)} %param.30, bf16[128,2,1024]{2,1,0:T(2,128)(2,1)S(1)} %all_to_all.20), kind=kOutput, calls=%fused_computation.14 | convolution fusion | flops 402653184 | bytes 2883584 | tf_op jit(solution)/shard_map/sekw,ewf->sekf/dot_general | solution.py:32
  106.2 0.4 convolution_convert_fusion
  106.7 1.4 %copy.43 = bf16[128,2,1024]{2,1,0:T(2,128)(2,1)} copy(bf16[128,2,1024]{2,0,1:T(8,128)(2,1)S(1)} %convolution_convert_fusion) | data formatting | bytes 1048576 | tf_op jit(solution)/shard_map/convert_element_type | solution.py:38
  108.0 5.3 %all-to-all-start.3 = ((bf16[128,2,1024]{2,1,0:T(2,128)(2,1)}), bf16[128,2,1024]{2,1,0:T(2,128)(2,1)}, u32[]{:S(2)}, u32[]{:S(2)}) async-start(bf16[128,2,1024]{2,1,0:T(2,128)(2,1)} %copy.43), calls=%async_computation.3 | async-start | bytes 1048576 | tf_op jit(solution)/shard_map/all_to_all | solution.py:63
  113.4 0.1 copy.39
  113.5 12.7 %all-to-all-done.3 = bf16[128,2,1024]{2,1,0:T(2,128)(2,1)} async-done(((bf16[128,2,1024]{2,1,0:T(2,128)(2,1)}), bf16[128,2,1024]{2,1,0:T(2,128)(2,1)}, u32[]{:S(2)}, u32[]{:S(2)}) %all-to-all-start.3) | async-done | bytes 524320 | tf_op jit(solution)/shard_map/all_to_all | solution.py:63
  126.2 2.1 %reshape.153 = bf16[256,1024]{1,0:T(8,128)(2,1)} reshape(bf16[128,2,1024]{2,1,0:T(2,128)(2,1)} %all-to-all-done.3) | data formatting | bytes 1048576 | tf_op jit(solution)/shard_map/reshape | solution.py:113
  128.3 2.2 %gather_fusion.2 = bf16[128,1024]{1,0:T(8,128)(2,1)S(1)} fusion(bf16[256,1024]{1,0:T(8,128)(2,1)} %reshape.153, s32[1024]{0:T(1024)S(1)} %pad_clamp_fusion), kind=kCustom, calls=%fused_computation.2 | custom fusion | bytes 524800 | tf_op jit(solution)/shard_map/gather | solution.py:113
  130.4 0.2 fusion.19
  130.6 0.6 add_convert_fusion
  (34 shorter events, 0.2 us)
Async XLA Ops:
  0.6 43.8 %copy-start = (bf16[1,768,2048]{2,1,0:T(8,128)(2,1)S(1)}, bf16[1,768,2048]{2,1,0:T(8,128)(2,1)}, u32[]{:S(2)}) copy-start(bf16[1,768,2048]{2,1,0:T(8,128)(2,1)} %param.22) | copy-start | bytes 9437188
  0.6 21.3 %copy-start.5 = (s32[16,8]{0,1:T(8,128)S(1)}, s32[16,8]{0,1:T(8,128)}, u32[]{:S(2)}) copy-start(s32[16,8]{0,1:T(8,128)} %param.27) | copy-start | bytes 1540
  0.7 21.5 %copy-start.3 = (f32[16,8]{0,1:T(8,128)S(1)}, f32[16,8]{0,1:T(8,128)}, u32[]{:S(2)}) copy-start(f32[16,8]{0,1:T(8,128)} %param.19) | copy-start | bytes 1540
  10.0 29.5 %all-to-all-start = ((bf16[128,2,2048]{2,1,0:T(2,128)(2,1)}), bf16[128,2,2048]{2,1,0:T(2,128)(2,1)}, u32[]{:S(2)}, u32[]{:S(2)}) async-start(bf16[128,2,2048]{2,1,0:T(2,128)(2,1)} %reshape.143), calls=%async_computation | async-start | bytes 2097152 | tf_op jit(solution)/shard_map/all_to_all | solution.py:51
  45.5 8.0 %copy-start.6 = (s32[16,8]{0,1:T(8,128)S(1)}, s32[16,8]{0,1:T(8,128)}, u32[]{:S(2)}) copy-start(s32[16,8]{0,1:T(8,128)} %param.20) | copy-start | bytes 1540
  45.5 8.5 %copy-start.10 = (s32[16]{0:T(128)S(1)}, s32[16]{0:T(128)}, u32[]{:S(2)}) copy-start(s32[16]{0:T(128)} %param.25) | copy-start | bytes 196
  47.6 23.5 %all-to-all-start.1 = ((bf16[128,2,2048]{2,1,0:T(2,128)(2,1)}), bf16[128,2,2048]{2,1,0:T(2,128)(2,1)}, u32[]{:S(2)}, u32[]{:S(2)}) async-start(bf16[128,2,2048]{2,1,0:T(2,128)(2,1)} %copy.38), calls=%async_computation.1 | async-start | bytes 2097152 | tf_op jit(solution)/shard_map/all_to_all | solution.py:49
  73.4 5.1 %copy-start.1 = (bf16[16,2048]{1,0:T(8,128)(2,1)S(1)}, bf16[16,2048]{1,0:T(8,128)(2,1)}, u32[]{:S(2)}) copy-start(bf16[16,2048]{1,0:T(8,128)(2,1)} %param.16) | copy-start | bytes 196612
  77.0 4.5 %copy-start.7 = (f32[1024]{0:T(1024)S(1)}, f32[1024]{0:T(1024)}, u32[]{:S(2)}) copy-start(f32[1024]{0:T(1024)} %param.26) | copy-start | bytes 12292
  78.5 25.6 %copy-start.2 = (bf16[16,2048]{1,0:T(8,128)(2,1)}, bf16[16,2048]{1,0:T(8,128)(2,1)S(1)}, u32[]{:S(2)}) copy-start(bf16[16,2048]{1,0:T(8,128)(2,1)S(1)} %fusion.36) | copy-start | bytes 196612
  85.6 20.5 %copy-start.9 = (bf16[1,384,1024]{2,1,0:T(8,128)(2,1)S(1)}, bf16[1,384,1024]{2,1,0:T(8,128)(2,1)}, u32[]{:S(2)}) copy-start(bf16[1,384,1024]{2,1,0:T(8,128)(2,1)} %param.31) | copy-start | bytes 2359300
  106.2 7.2 %copy-start.4 = (f32[16,8]{0,1:T(8,128)S(1)}, f32[16,8]{0,1:T(8,128)}, u32[]{:S(2)}) copy-start(f32[16,8]{0,1:T(8,128)} %param.28) | copy-start | bytes 1540
  106.2 7.2 %copy-start.8 = (s32[16,8]{0,1:T(8,128)S(1)}, s32[16,8]{0,1:T(8,128)}, u32[]{:S(2)}) copy-start(s32[16,8]{0,1:T(8,128)} %param.29) | copy-start | bytes 1540
  108.0 18.2 %all-to-all-start.3 = ((bf16[128,2,1024]{2,1,0:T(2,128)(2,1)}), bf16[128,2,1024]{2,1,0:T(2,128)(2,1)}, u32[]{:S(2)}, u32[]{:S(2)}) async-start(bf16[128,2,1024]{2,1,0:T(2,128)(2,1)} %copy.43), calls=%async_computation.3 | async-start | bytes 1048576 | tf_op jit(solution)/shard_map/all_to_all | solution.py:63
where the time goes:
time: 132 us; the launch traced here: 131 us
  waiting for transfers between devices  42.7 us (32%)
  local copies, waits for them, and re-layouts  28.5 us (22%)
  starting transfers between devices  23.2 us (18%)
  blocking collectives  18.5 us (14%)
  matrix products  11.4 us (9%)
  other arithmetic  6.04 us (5%)
    all_to_all x1, blocking collectives, talk_layer(): lax.all_to_all(bin_rows, ('grp', 'dp', 'ep'), split_axis=0, concat_axis=0...  18.5 us
    all_to_all x1, waiting for transfers between devices, think_layer(): lax.all_to_all(bin_rows, ('grp', 'dp', 'ep'), split_axis=0, concat_axis=0...  17.3 us
    all_to_all x1, waiting for transfers between devices, talk_layer(): lax.all_to_all(run_experts(lax.all_to_all(bin_rows, ('grp', 'dp', 'ep'),...  12.7 us
    all_to_all x1, waiting for transfers between devices, think_layer(): lax.all_to_all(run_experts(lax.all_to_all(bin_rows, ('grp', 'dp', 'ep'),...  12.7 us
    all_to_all x1, starting transfers between devices, think_layer(): lax.all_to_all(bin_rows, ('grp', 'dp', 'ep'), split_axis=0, concat_axis=0...  12 us
    dot_general x2, matrix products, run_experts(): jnp.einsum('sekw,ewf->sekf', grouped, gate_up, preferred_element_type=jnp...  6.9 us
    all_to_all x1, starting transfers between devices, think_layer(): lax.all_to_all(run_experts(lax.all_to_all(bin_rows, ('grp', 'dp', 'ep'),...  5.89 us
    all_to_all x1, starting transfers between devices, talk_layer(): lax.all_to_all(run_experts(lax.all_to_all(bin_rows, ('grp', 'dp', 'ep'),...  5.33 us
  transfers between devices with their start and end apart: 3, of which 3 were waited for; matrix products, arithmetic and copies ran while one was open for 4% of the time, Pallas kernels for 0%

commit v1 on v0

v1 whole, which is shorter than its diff:
```python
import functools

import jax
import jax.numpy as jnp
import numpy as np
from jax import lax
from jax.experimental import pallas as pl
from jax.experimental.pallas import tpu as pltpu
from jax.sharding import PartitionSpec as P

MESH = pl.DeviceIdType.MESH
AXES = ("grp", "dp", "ep")
ROWS = 16
SLOT = 16
PARTNERS = 128
F32 = jnp.float32
BF16 = jnp.bfloat16


def partner_order():
    rng = np.random.default_rng(1)
    every = [(a, c, p, q) for a in range(2) for c in range(4) for p in range(4) for q in range(4)]
    shuffled = [every[i] for i in rng.permutation(len(every))]

    def hops(step):
        return sum(min(v, 4 - v) for v in step[1:]) + (0 if any(step) else -1)

    return sorted(shuffled, key=lambda step: -hops(step))


ORDER = partner_order()
CHUNKS = ((0, 128),)


def my_place():
    ep = lax.axis_index("ep")
    return lax.axis_index("grp"), lax.axis_index("dp"), ep // 4, ep % 4


def device_at(place, step, sign):
    grp, dp, x, y = place
    a, c, p, q = step
    if sign < 0:
        a, c, p, q = (-a) % 2, (-c) % 4, (-p) % 4, (-q) % 4
    return ((grp + a) % 2, (dp + c) % 4, ((x + p) % 4) * 4 + (y + q) % 4)


def iota(shape, dim):
    return lax.broadcasted_iota(jnp.int32, shape, dim)


def dot(a, b):
    return jnp.dot(a, b, preferred_element_type=F32)


def rms_rows(values, gain):
    inverse = lax.rsqrt(jnp.mean(values * values, axis=-1, keepdims=True) + 1e-06)
    return (values * inverse * gain).astype(BF16)


def route_tables(place, steps, routes, weights, keep, pick_ref, mix_ref):
    grp, dp, x, y = place
    expert = (
        (((grp + steps // 64) & 1) * 4 + ((dp + (steps // 16) % 4) & 3)) * 16
        + ((x + (steps // 4) % 4) & 3) * 4
        + ((y + steps % 4) & 3)
    )
    shares = weights * keep.astype(F32) / jnp.sum(weights, axis=1, keepdims=True)
    named = jnp.zeros((ROWS, PARTNERS), F32)
    share = jnp.zeros((ROWS, PARTNERS), F32)
    for k in range(routes.shape[1]):
        match = routes[:, k : k + 1] == expert
        named = named + jnp.where(match, 1.0, 0.0)
        share = share + jnp.where(match, shares[:, k : k + 1], 0.0)
    below = (iota((ROWS, ROWS), 1) < iota((ROWS, ROWS), 0)).astype(F32).astype(BF16)
    code = named * (1.0 + dot(below, named.astype(BF16)))
    high = share.astype(BF16)
    low = (share - high.astype(F32)).astype(BF16)
    wide = PARTNERS * SLOT
    spread = jnp.where(iota((PARTNERS, wide), 1) // SLOT == iota((PARTNERS, wide), 0), 1.0, 0.0).astype(BF16)
    stacked = jnp.concatenate([code.astype(BF16), high, low], axis=0)
    lanes = dot(stacked, spread)
    lane = iota((ROWS, wide), 1)
    chosen = lanes[:ROWS] == ((lane & 1) + 1).astype(F32)
    parts = (
        jnp.where(chosen, 1.0, 0.0),
        jnp.where(chosen, lanes[ROWS : 2 * ROWS], 0.0),
        jnp.where(chosen, lanes[2 * ROWS :], 0.0),
    )
    block = (lane >> 1) & 7
    for c in range(8):
        here = block == c
        pick_ref[c * ROWS : (c + 1) * ROWS, :] = jnp.where(here, parts[0], 0.0).astype(BF16)
        mix_ref[c * ROWS : (c + 1) * ROWS, :] = jnp.where(here, parts[1], 0.0).astype(BF16)
        mix_ref[128 + c * ROWS : 128 + (c + 1) * ROWS, :] = jnp.where(here, parts[2], 0.0).astype(BF16)


def by_blocks(rows, halves):
    return jnp.concatenate(
        [
            jnp.concatenate(
                [rows[:, h * 1024 + c * 128 : h * 1024 + (c + 1) * 128] for h in range(halves)], axis=1
            )
            for c in range(8)
        ],
        axis=0,
    )


def unblock(blocks, halves):
    return jnp.concatenate(
        [
            blocks[c * ROWS : (c + 1) * ROWS, h * 128 : (h + 1) * 128]
            for h in range(halves)
            for c in range(8)
        ],
        axis=1,
    )


def copy_to(source, target, device, send_sem, recv_sem):
    return pltpu.make_async_remote_copy(
        src_ref=source,
        dst_ref=target,
        send_sem=send_sem,
        recv_sem=recv_sem,
        device_id=device,
        device_id_type=MESH,
    )


def wait_bytes(ref, first, last, sem):
    part = ref.at[pl.ds(first * SLOT, (last - first) * SLOT)]
    pltpu.make_async_copy(part, part, sem).wait()


def expert_layer(place, normed, halves, pick, mix, gate_up, down, wait_weights, idle, bufs, sems):
    bins, arrived, rows, hidden, results, packed, returned = bufs
    there_send, there_recv, back_send, back_recv = sems
    width = halves * 1024
    blocks = by_blocks(normed, halves)
    for g in range(8):
        lanes = pl.ds(g * 256, 256)
        bins[lanes, :] = lax.dot_general(
            pick[:, lanes], blocks, (((0,), (0,)), ((), ())), preferred_element_type=F32
        ).astype(BF16)
        for j in range(g * 16, min(g * 16 + 16, PARTNERS - 1)):
            part = pl.ds(j * SLOT, SLOT)
            copy_to(
                bins.at[part], arrived.at[part], device_at(place, ORDER[j], 1), there_send, there_recv.at[chunk_of(j)]
            ).start()
    own = pl.ds((PARTNERS - 1) * SLOT, SLOT)
    arrived[own, :] = bins[own, :]

    out_row, in_row = iota((256, 256), 0), iota((256, 256), 1)
    unpack = jnp.where(((out_row // 2) % 16) * 16 + (out_row // 32) * 2 + out_row % 2 == in_row, 1.0, 0.0).astype(BF16)
    pack = jnp.where(((in_row // 2) % 16) * 16 + (in_row // 32) * 2 + in_row % 2 == out_row, 1.0, 0.0).astype(BF16)
    hidden_width = down.shape[1]
    idle()
    wait_weights()
    for k, (first, last) in enumerate(CHUNKS):
        wait_bytes(arrived, first, min(last, PARTNERS - 1), there_recv.at[k])
        for g in range(first // 16, last // 16):
            group = dot(unpack, arrived[g * 256 : (g + 1) * 256, :]).astype(BF16)
            for h in range(halves):
                for c in range(8):
                    rows[g * 32 : (g + 1) * 32, h * 1024 + c * 128 : h * 1024 + (c + 1) * 128] = group[
                        c * 32 : (c + 1) * 32, h * 128 : (h + 1) * 128
                    ]
        span = slice(first * 2, last * 2)
        tile = 256 if hidden_width % 256 == 0 else 128
        for n in range(hidden_width // tile):
            gate = dot(rows[span, :], gate_up[0, :, n * tile : (n + 1) * tile])
            up = dot(rows[span, :], gate_up[0, :, hidden_width + n * tile : hidden_width + (n + 1) * tile])
            hidden[span, n * tile : (n + 1) * tile] = (gate / (1.0 + jnp.exp(-gate)) * up).astype(BF16)
        for n in range(width // 256):
            results[span, n * 256 : (n + 1) * 256] = dot(
                hidden[span, :], down[0, :, n * 256 : (n + 1) * 256]
            ).astype(BF16)
        for g in range(first // 16, last // 16):
            stacked = jnp.concatenate(
                [
                    jnp.concatenate(
                        [
                            results[g * 32 : (g + 1) * 32, h * 1024 + c * 128 : h * 1024 + (c + 1) * 128]
                            for h in range(halves)
                        ],
                        axis=1,
                    )
                    for c in range(8)
                ],
                axis=0,
            )
            packed[g * 256 : (g + 1) * 256, :] = dot(pack, stacked).astype(BF16)
            for j in range(g * 16, min(g * 16 + 16, PARTNERS - 1)):
                part = pl.ds(j * SLOT, SLOT)
                copy_to(
                    packed.at[part], returned.at[part], device_at(place, ORDER[j], -1), back_send, back_recv
                ).start()
    returned[own, :] = packed[own, :]
    wait_bytes(returned, 0, PARTNERS - 1, back_recv)
    total = dot(mix[...], returned[...])
    wait_bytes(bins, 0, PARTNERS - 1, there_send)
    wait_bytes(packed, 0, PARTNERS - 1, back_send)
    return unblock(total[:128] + total[128:], halves)


def chunk_of(j):
    return next(k for k, (first, last) in enumerate(CHUNKS) if first <= j < last)


def step_kernel(
    steps,
    tokens,
    think_gain,
    think_routes,
    think_weights,
    think_keep,
    codec_ids,
    talk_gain,
    talk_routes,
    talk_weights,
    talk_keep,
    think_gate_up,
    think_down,
    talk_proj,
    codec_table,
    talk_gate_up,
    talk_down,
    think_out,
    talk_out,
    gu1,
    dn1,
    proj,
    table,
    gu2,
    dn2,
    codec,
    pick1,
    mix1,
    pick2,
    mix2,
    bins1,
    arrived1,
    rows1,
    hidden1,
    results1,
    packed1,
    returned1,
    bins2,
    arrived2,
    rows2,
    hidden2,
    results2,
    packed2,
    returned2,
    load_sem,
    send_sem,
    there_recv,
    back_recv,
):
    place = my_place()
    barrier = pltpu.get_barrier_semaphore()
    for step in ORDER[:-1]:
        pl.semaphore_signal(barrier, inc=1, device_id=device_at(place, step, 1), device_id_type=MESH)

    loads = [
        pltpu.make_async_copy(source, target, load_sem.at[i])
        for i, (source, target) in enumerate(
            (
                (think_gate_up, gu1),
                (think_down, dn1),
                (codec_table, table),
                (talk_proj, proj),
                (talk_gate_up, gu2),
                (talk_down, dn2),
            )
        )
    ]
    for load in loads:
        load.start()

    partner = steps[...]
    normed = rms_rows(tokens[...].astype(F32), think_gain[...])
    route_tables(place, partner, think_routes[...], think_weights[...], think_keep[...], pick1, mix1)
    route_tables(place, partner, talk_routes[...], talk_weights[...], talk_keep[...], pick2, mix2)
    pl.semaphore_wait(barrier, PARTNERS - 1)

    def find_codec():
        loads[2].wait()
        vocab = table.shape[0]
        row = iota((ROWS, vocab), 0)
        ids = jnp.zeros((ROWS, vocab), jnp.int32)
        for t in range(ROWS):
            ids = jnp.where(row == t, codec_ids[t], ids)
        chosen = jnp.where(iota((ROWS, vocab), 1) == ids, 1.0, 0.0).astype(BF16)
        codec[...] = dot(chosen, table[...])

    def think_weights_ready():
        loads[0].wait()
        loads[1].wait()

    mixed = expert_layer(
        place,
        normed,
        2,
        pick1,
        mix1,
        gu1,
        dn1,
        think_weights_ready,
        find_codec,
        (bins1, arrived1, rows1, hidden1, results1, packed1, returned1),
        (send_sem.at[0], there_recv.at[0], send_sem.at[1], back_recv.at[0]),
    )
    think = (tokens[...].astype(F32) + mixed).astype(BF16)
    think_out[...] = think

    loads[3].wait()
    talk_input = dot(think, proj[...]) + codec[...]
    talk_normed = rms_rows(talk_input, talk_gain[...])

    def talk_weights_ready():
        loads[4].wait()
        loads[5].wait()

    mixed = expert_layer(
        place,
        talk_normed,
        1,
        pick2,
        mix2,
        gu2,
        dn2,
        talk_weights_ready,
        lambda: None,
        (bins2, arrived2, rows2, hidden2, results2, packed2, returned2),
        (send_sem.at[2], there_recv.at[1], send_sem.at[3], back_recv.at[1]),
    )
    talk_out[...] = (talk_input + mixed).astype(BF16)


def shards(
    tokens,
    think_gain,
    think_routes,
    think_weights,
    think_keep,
    think_gate_up,
    think_down,
    talk_proj,
    codec_table,
    codec_ids,
    talk_gain,
    talk_routes,
    talk_weights,
    talk_keep,
    talk_gate_up,
    talk_down,
):
    steps = jnp.asarray([[((a * 4 + c) * 4 + p) * 4 + q for a, c, p, q in ORDER]], jnp.int32)
    wide = PARTNERS * SLOT
    vmem = pl.BlockSpec(memory_space=pltpu.VMEM)
    smem = pl.BlockSpec(memory_space=pltpu.SMEM)
    hbm = pl.BlockSpec(memory_space=pl.ANY)

    def exchange(halves, hidden_width):
        width = halves * 1024
        return [
            pltpu.VMEM((wide, halves * 128), BF16),
            pltpu.VMEM((wide, halves * 128), BF16),
            pltpu.VMEM((256, width), BF16),
            pltpu.VMEM((256, hidden_width), BF16),
            pltpu.VMEM((256, width), BF16),
            pltpu.VMEM((wide, halves * 128), BF16),
            pltpu.VMEM((wide, halves * 128), BF16),
        ]

    return pl.pallas_call(
        step_kernel,
        out_shape=(
            jax.ShapeDtypeStruct(tokens.shape, BF16),
            jax.ShapeDtypeStruct((ROWS, talk_proj.shape[1]), BF16),
        ),
        in_specs=[vmem] * 6 + [smem] + [vmem] * 4 + [hbm] * 6,
        out_specs=(vmem, vmem),
        scratch_shapes=[
            pltpu.VMEM(think_gate_up.shape, BF16),
            pltpu.VMEM(think_down.shape, BF16),
            pltpu.VMEM(talk_proj.shape, BF16),
            pltpu.VMEM(codec_table.shape, BF16),
            pltpu.VMEM(talk_gate_up.shape, BF16),
            pltpu.VMEM(talk_down.shape, BF16),
            pltpu.VMEM((ROWS, talk_proj.shape[1]), F32),
            pltpu.VMEM((128, wide), BF16),
            pltpu.VMEM((256, wide), BF16),
            pltpu.VMEM((128, wide), BF16),
            pltpu.VMEM((256, wide), BF16),
        ]
        + exchange(2, think_down.shape[1])
        + exchange(1, talk_down.shape[1])
        + [
            pltpu.SemaphoreType.DMA((6,)),
            pltpu.SemaphoreType.DMA((4,)),
            pltpu.SemaphoreType.DMA((2, len(CHUNKS))),
            pltpu.SemaphoreType.DMA((2,)),
        ],
        compiler_params=pltpu.CompilerParams(
            collective_id=0, has_side_effects=True, vmem_limit_bytes=56 * 2**20
        ),
        name="moe_step",
    )(
        steps,
        tokens,
        think_gain.reshape(1, -1),
        think_routes,
        think_weights,
        think_keep,
        codec_ids,
        talk_gain.reshape(1, -1),
        talk_routes,
        talk_weights,
        talk_keep,
        think_gate_up,
        think_down,
        talk_proj,
        codec_table,
        talk_gate_up,
        talk_down,
    )


def solution(mesh):
    rows = P(AXES, None)
    experts = P(AXES, None, None)
    return jax.shard_map(
        shards,
        mesh=mesh,
        in_specs=(rows, P(), rows, rows, rows, experts, experts, P(), P(), P(AXES), P(), rows, rows, rows, experts, experts),
        out_specs=(rows, rows),
        check_vma=False,
    )
```

time: 132 us -> 79.2 us (0.60)
  Pallas kernels: 0 us -> 67.1 us
  waiting for transfers between devices: 42.7 us -> 0 us
  starting transfers between devices: 23.2 us -> 0 us
  blocking collectives: 18.5 us -> 0 us
  local copies, waits for them, and re-layouts: 28.5 us -> 11 us
  matrix products: 11.4 us -> 0 us
  other arithmetic: 6.04 us -> 0 us
    pallas_call x0 -> x1, Pallas kernels: none -> 67.1 us  [shards(): pl.pallas_call(step_kernel, out_shape=(jax.ShapeDtypeStruct(tokens.shape,...]
    all_to_all x3 -> x0, waiting for transfers between devices: 42.7 us -> none  [the longest x1 17.3 us: think_layer(): lax.all_to_all(bin_rows, ('grp', 'dp', 'ep'), split_axis=0, concat_axis=0...]
    all_to_all x3 -> x0, starting transfers between devices: 23.2 us -> none  [the longest x1 12 us: think_layer(): lax.all_to_all(bin_rows, ('grp', 'dp', 'ep'), split_axis=0, concat_axis=0...]
    all_to_all x1 -> x0, blocking collectives: 18.5 us -> none  [talk_layer(): lax.all_to_all(bin_rows, ('grp', 'dp', 'ep'), split_axis=0, concat_axis=0...]
    dot_general x5 -> x0, matrix products: 11.4 us -> none  [the longest x2 6.9 us: run_experts(): jnp.einsum('sekw,ewf->sekf', grouped, gate_up, preferred_element_type=jnp...]
    gather x3 -> x0, local copies, waits for them, and re-layouts: 9.98 us -> none  [the longest x1 4.21 us: shards(): codec_table[codec_ids].astype(jnp.float32)]
    unnamed x24 -> x8, local copies, waits for them, and re-layouts: 1.04 us -> 11 us
    reshape x4 -> x0, local copies, waits for them, and re-layouts: 8.92 us -> none  [the longest x2 4.59 us: fill_bins(): return (bin_rows.reshape(expert_count, capacity, row_width), positions)]
  transfers between devices with their start and end apart: 3 -> 0, of which waited for: 3 -> 0; matrix products, arithmetic and copies ran while one was open for 4% -> 0% of each run, Pallas kernels for 0% -> 0%
where the time goes in v1:
time: 79.2 us; the launch traced here: 78.8 us
  Pallas kernels  67.1 us (85%)
  local copies, waits for them, and re-layouts  11 us (14%)
    pallas_call x1, Pallas kernels, shards(): pl.pallas_call(step_kernel, out_shape=(jax.ShapeDtypeStruct(tokens.shape,...  67.1 us
    unnamed x8, local copies, waits for them, and re-layouts  11 us

profile of v1, /device:TPU:1, one launch (start us, length us, event | category | flops | bytes accessed | tf_op | source)
XLA Modules:
  0.0 78.8 jit_solution(11500148899753537882)
XLA Ops:
  0.6 1.4 %copy.19.think_routes = s32[16,8]{1,0:T(8,128)} copy(s32[16,8]{0,1:T(8,128)} %param.19) | data formatting | bytes 1024 | tf_op args[2]
  2.0 1.4 %copy.20.think_weights = f32[16,8]{1,0:T(8,128)} copy(f32[16,8]{0,1:T(8,128)} %param.20) | data formatting | bytes 1024 | tf_op args[3]
  3.3 1.4 %copy.21.think_keep = s32[16,8]{1,0:T(8,128)} copy(s32[16,8]{0,1:T(8,128)} %param.21) | data formatting | bytes 1024 | tf_op args[4]
  4.7 1.4 %copy.22.talk_routes = s32[16,8]{1,0:T(8,128)} copy(s32[16,8]{0,1:T(8,128)} %param.28) | data formatting | bytes 1024 | tf_op args[11]
  6.0 1.4 %copy.23.talk_weights = f32[16,8]{1,0:T(8,128)} copy(f32[16,8]{0,1:T(8,128)} %param.29) | data formatting | bytes 1024 | tf_op args[12]
  7.4 1.4 %copy.24.talk_keep = s32[16,8]{1,0:T(8,128)} copy(s32[16,8]{0,1:T(8,128)} %param.30) | data formatting | bytes 1024 | tf_op args[13]
  8.8 67.1 %moe_step.1 = (bf16[16,2048]{1,0:T(8,128)(2,1)}, bf16[16,1024]{1,0:T(8,128)(2,1)}) custom-call(s32[1,128]{1,0:T(1,128)} %constant.2.clone.steps, bf16[16,2048]{1,0:T(8,128)(2,1)} %tokens.1, f32[1,2048]{1,0:T(1,128)} %bitcast.2, s32[16,8]{1,0:T(8,128)} %copy.19.think_routes, f32[16,8]{1,0:T(8,128)} %copy.20.think_weights, s32[16,8]{1,0:T(8,128)} %copy.21.think_keep, ...), custom_call_target="tpu_custom_call" | custom-call | tf_op jit(solution)/shard_map/moe_step/pallas_call | solution.py:379
  75.9 1.5 %copy.27 = bf16[16,2048]{1,0:T(8,128)(2,1)} copy(bf16[16,2048]{1,0:T(8,128)(2,1)} %get-tuple-element.4) | data formatting | bytes 131072
  77.4 1.4 %copy.28 = bf16[16,1024]{1,0:T(8,128)(2,1)} copy(bf16[16,1024]{1,0:T(8,128)(2,1)} %get-tuple-element.5) | data formatting | bytes 65536

commit v2 on v1

v2 whole, which is shorter than its diff:
```python
import functools

import jax
import jax.numpy as jnp
import numpy as np
from jax import lax
from jax.experimental import pallas as pl
from jax.experimental.pallas import tpu as pltpu
from jax.sharding import PartitionSpec as P

MESH = pl.DeviceIdType.MESH
AXES = ("grp", "dp", "ep")
ROWS = 16
SLOT = 16
PARTNERS = 128
F32 = jnp.float32
BF16 = jnp.bfloat16


def hops(step):
    return sum(min(v, 4 - v) for v in step[1:])


def partner_order(distances):
    rng = np.random.default_rng(1)
    every = [(a, c, p, q) for a in range(2) for c in range(4) for p in range(4) for q in range(4)]
    shuffled = [every[i] for i in rng.permutation(len(every))]
    return sorted(shuffled, key=lambda step: distances.index(hops(step)) if any(step) else len(distances))


THINK_ORDER = partner_order((3, 6, 5, 4, 2, 1, 0))
TALK_ORDER = partner_order((6, 5, 4, 3, 2, 1, 0))
EARLY = sum(hops(step) == 3 for step in THINK_ORDER)
THINK_CHUNKS = ((0, 48), (48, 128))
TALK_CHUNKS = ((0, 48), (48, 128))
NEAR = [step for step in THINK_ORDER[:-1] if hops(step) <= 3]
RELAYS = ((0, 1, 1, 1), (0, 3, 3, 3))


def my_place():
    ep = lax.axis_index("ep")
    return lax.axis_index("grp"), lax.axis_index("dp"), ep // 4, ep % 4


def device_at(place, step, sign):
    grp, dp, x, y = place
    a, c, p, q = step
    if sign < 0:
        a, c, p, q = (-a) % 2, (-c) % 4, (-p) % 4, (-q) % 4
    return ((grp + a) % 2, (dp + c) % 4, ((x + p) % 4) * 4 + (y + q) % 4)


def iota(shape, dim):
    return lax.broadcasted_iota(jnp.int32, shape, dim)


def dot(a, b):
    return jnp.dot(a, b, preferred_element_type=F32)


def rms_rows(values, gain):
    inverse = lax.rsqrt(jnp.mean(values * values, axis=-1, keepdims=True) + 1e-06)
    return (values * inverse * gain).astype(BF16)


def route_tables(place, steps, routes, weights, keep, pick_ref, mix_ref):
    grp, dp, x, y = place
    expert = (
        (((grp + steps // 64) & 1) * 4 + ((dp + (steps // 16) % 4) & 3)) * 16
        + ((x + (steps // 4) % 4) & 3) * 4
        + ((y + steps % 4) & 3)
    )
    shares = jnp.transpose(weights * keep.astype(F32) / jnp.sum(weights, axis=0, keepdims=True))
    routes = jnp.transpose(routes)
    named = jnp.zeros((ROWS, PARTNERS), F32)
    share = jnp.zeros((ROWS, PARTNERS), F32)
    for k in range(routes.shape[1]):
        match = routes[:, k : k + 1] == expert
        named = named + jnp.where(match, 1.0, 0.0)
        share = share + jnp.where(match, shares[:, k : k + 1], 0.0)
    below = (iota((ROWS, ROWS), 1) < iota((ROWS, ROWS), 0)).astype(F32).astype(BF16)
    code = named * (1.0 + dot(below, named.astype(BF16)))
    high = share.astype(BF16)
    low = (share - high.astype(F32)).astype(BF16)
    wide = PARTNERS * SLOT
    spread = jnp.where(iota((PARTNERS, wide), 1) // SLOT == iota((PARTNERS, wide), 0), 1.0, 0.0).astype(BF16)
    stacked = jnp.concatenate([code.astype(BF16), high, low], axis=0)
    lanes = dot(stacked, spread)
    lane = iota((ROWS, wide), 1)
    chosen = lanes[:ROWS] == ((lane & 1) + 1).astype(F32)
    parts = (
        jnp.where(chosen, 1.0, 0.0),
        jnp.where(chosen, lanes[ROWS : 2 * ROWS], 0.0),
        jnp.where(chosen, lanes[2 * ROWS :], 0.0),
    )
    block = (lane >> 1) & 7
    for c in range(8):
        here = block == c
        pick_ref[c * ROWS : (c + 1) * ROWS, :] = jnp.where(here, parts[0], 0.0).astype(BF16)
        mix_ref[c * ROWS : (c + 1) * ROWS, :] = jnp.where(here, parts[1], 0.0).astype(BF16)
        mix_ref[128 + c * ROWS : 128 + (c + 1) * ROWS, :] = jnp.where(here, parts[2], 0.0).astype(BF16)


def by_blocks(rows, halves):
    return jnp.concatenate(
        [
            jnp.concatenate(
                [rows[:, h * 1024 + c * 128 : h * 1024 + (c + 1) * 128] for h in range(halves)], axis=1
            )
            for c in range(8)
        ],
        axis=0,
    )


def unblock(blocks, halves):
    return jnp.concatenate(
        [
            blocks[c * ROWS : (c + 1) * ROWS, h * 128 : (h + 1) * 128]
            for h in range(halves)
            for c in range(8)
        ],
        axis=1,
    )


def copy_to(source, target, device, send_sem, recv_sem):
    return pltpu.make_async_remote_copy(
        src_ref=source,
        dst_ref=target,
        send_sem=send_sem,
        recv_sem=recv_sem,
        device_id=device,
        device_id_type=MESH,
    )


def wait_bytes(ref, first, last, sem):
    part = ref.at[pl.ds(first * SLOT, (last - first) * SLOT)]
    pltpu.make_async_copy(part, part, sem).wait()


def send_bins(place, order, bins, arrived, slots, chunks, send_sem, recv_sems):
    for j in slots:
        part = pl.ds(j * SLOT, SLOT)
        copy_to(
            bins.at[part], arrived.at[part], device_at(place, order[j], 1), send_sem, recv_sems.at[chunk_of(j, chunks)]
        ).start()


def chunk_of(j, chunks):
    return next(k for k, (first, last) in enumerate(chunks) if first <= j < last)


def fill_bins(g, pick, blocks, bins):
    lanes = pl.ds(g * 256, 256)
    bins[lanes, :] = lax.dot_general(
        pick[:, lanes], blocks, (((0,), (0,)), ((), ())), preferred_element_type=F32
    ).astype(BF16)


def run_expert(place, order, chunks, halves, mix, gate_up, down, bufs, sems):
    bins, arrived, rows, hidden, results, packed, returned = bufs
    there_recv, back_send, back_recv = sems
    width = halves * 1024
    own = pl.ds((PARTNERS - 1) * SLOT, SLOT)
    arrived[own, :] = bins[own, :]

    out_row, in_row = iota((256, 256), 0), iota((256, 256), 1)
    unpack = jnp.where(((out_row // 2) % 16) * 16 + (out_row // 32) * 2 + out_row % 2 == in_row, 1.0, 0.0).astype(BF16)
    pack = jnp.where(((in_row // 2) % 16) * 16 + (in_row // 32) * 2 + in_row % 2 == out_row, 1.0, 0.0).astype(BF16)
    hidden_width = down.shape[1]
    for k, (first, last) in enumerate(chunks):
        wait_bytes(arrived, first, min(last, PARTNERS - 1), there_recv.at[k])
        for g in range(first // 16, last // 16):
            group = dot(unpack, arrived[g * 256 : (g + 1) * 256, :]).astype(BF16)
            for h in range(halves):
                for c in range(8):
                    rows[g * 32 : (g + 1) * 32, h * 1024 + c * 128 : h * 1024 + (c + 1) * 128] = group[
                        c * 32 : (c + 1) * 32, h * 128 : (h + 1) * 128
                    ]
        span = slice(first * 2, last * 2)
        tile = 256 if hidden_width % 256 == 0 else 128
        for n in range(hidden_width // tile):
            gate = dot(rows[span, :], gate_up[0, :, n * tile : (n + 1) * tile])
            up = dot(rows[span, :], gate_up[0, :, hidden_width + n * tile : hidden_width + (n + 1) * tile])
            hidden[span, n * tile : (n + 1) * tile] = (gate / (1.0 + jnp.exp(-gate)) * up).astype(BF16)
        for n in range(width // 256):
            results[span, n * 256 : (n + 1) * 256] = dot(
                hidden[span, :], down[0, :, n * 256 : (n + 1) * 256]
            ).astype(BF16)
        for g in range(first // 16, last // 16):
            stacked = jnp.concatenate(
                [
                    jnp.concatenate(
                        [
                            results[g * 32 : (g + 1) * 32, h * 1024 + c * 128 : h * 1024 + (c + 1) * 128]
                            for h in range(halves)
                        ],
                        axis=1,
                    )
                    for c in range(8)
                ],
                axis=0,
            )
            packed[g * 256 : (g + 1) * 256, :] = dot(pack, stacked).astype(BF16)
            for j in range(g * 16, min(g * 16 + 16, PARTNERS - 1)):
                part = pl.ds(j * SLOT, SLOT)
                copy_to(packed.at[part], returned.at[part], device_at(place, order[j], -1), back_send, back_recv).start()
    returned[own, :] = packed[own, :]
    wait_bytes(returned, 0, PARTNERS - 1, back_recv)
    total = dot(mix[...], returned[...])
    return unblock(total[:128] + total[128:], halves)


def step_kernel(*refs):
    small, (gate_up1, down1, table_hbm, proj_hbm, gate_up2, down2) = refs[:11], refs[11:17]
    think_out, talk_out = refs[17:19]
    here, (gu1, dn1, table, proj, gu2, dn2) = refs[19:30], refs[30:36]
    think_row, talk_row, pick1, mix1, pick2, mix2 = refs[36:42]
    think_bufs, talk_bufs = refs[42:49], refs[49:56]
    small_sem, load_sem, send_sem, there_recv, back_recv, out_sem, relay_sem = refs[56:]
    steps, tokens, gain1, routes1, weights1, keep1, codec_ids, gain2, routes2, weights2, keep2 = here

    place = my_place()
    barrier = pltpu.get_barrier_semaphore()
    for step in NEAR:
        pl.semaphore_signal(barrier, inc=1, device_id=device_at(place, step, 1), device_id_type=MESH)
    smalls = [pltpu.make_async_copy(a, b, small_sem.at[i]) for i, (a, b) in enumerate(zip(small, here))]
    loads = [
        pltpu.make_async_copy(a, b, load_sem.at[i])
        for i, (a, b) in enumerate(
            zip((gate_up1, down1, table_hbm, proj_hbm, gate_up2, down2), (gu1, dn1, table, proj, gu2, dn2))
        )
    ]
    for load in smalls + loads:
        load.start()
    for load in smalls:
        load.wait()

    normed = rms_rows(tokens[...].astype(F32), gain1[...])
    route_tables(place, steps[0:1, :], routes1[...], weights1[...], keep1[...], pick1, mix1)
    bins, arrived = think_bufs[:2]
    blocks = by_blocks(normed, 2)
    for g in range(8):
        fill_bins(g, pick1, blocks, bins)
    pl.semaphore_wait(barrier, len(NEAR))
    for step in RELAYS:
        pl.semaphore_signal(relay_sem, inc=1, device_id=device_at(place, step, 1), device_id_type=MESH)
    send = functools.partial(send_bins, place, THINK_ORDER, bins, arrived)
    send(range(EARLY), THINK_CHUNKS, send_sem.at[0], there_recv.at[0])
    pl.semaphore_wait(relay_sem, len(RELAYS))
    send(range(EARLY, PARTNERS - 1), THINK_CHUNKS, send_sem.at[0], there_recv.at[0])

    route_tables(place, steps[1:2, :], routes2[...], weights2[...], keep2[...], pick2, mix2)
    loads[2].wait()
    vocab = table.shape[0]
    ids = jnp.transpose(jnp.broadcast_to(codec_ids[...], (8, ROWS)))[:, :1]
    chosen = jnp.where(iota((ROWS, vocab), 1) == ids, 1.0, 0.0).astype(BF16)
    codec = dot(chosen, table[...])
    loads[0].wait()
    loads[1].wait()
    mixed = run_expert(
        place,
        THINK_ORDER,
        THINK_CHUNKS,
        2,
        mix1,
        gu1,
        dn1,
        think_bufs,
        (there_recv.at[0], send_sem.at[1], back_recv.at[0]),
    )
    think = (tokens[...].astype(F32) + mixed).astype(BF16)
    think_row[...] = think
    think_store = pltpu.make_async_copy(think_row, think_out, out_sem.at[0])
    think_store.start()

    loads[3].wait()
    talk_input = dot(think, proj[...]) + codec
    blocks = by_blocks(rms_rows(talk_input, gain2[...]), 1)
    bins, arrived = talk_bufs[:2]
    for g in range(8):
        fill_bins(g, pick2, blocks, bins)
        slots = range(g * 16, min(g * 16 + 16, PARTNERS - 1))
        send_bins(place, TALK_ORDER, bins, arrived, slots, TALK_CHUNKS, send_sem.at[2], there_recv.at[1])
    loads[4].wait()
    loads[5].wait()
    mixed = run_expert(
        place,
        TALK_ORDER,
        TALK_CHUNKS,
        1,
        mix2,
        gu2,
        dn2,
        talk_bufs,
        (there_recv.at[1], send_sem.at[3], back_recv.at[1]),
    )
    talk_row[...] = (talk_input + mixed).astype(BF16)
    talk_store = pltpu.make_async_copy(talk_row, talk_out, out_sem.at[1])
    talk_store.start()
    for i, sent in enumerate((think_bufs[0], think_bufs[5], talk_bufs[0], talk_bufs[5])):
        wait_bytes(sent, 0, PARTNERS - 1, send_sem.at[i])
    think_store.wait()
    talk_store.wait()


def hand_over(think_in, talk_in, think_out, talk_out):
    think_out[...] = think_in[...]
    talk_out[...] = talk_in[...]


def shards(
    tokens,
    think_gain,
    think_routes,
    think_weights,
    think_keep,
    think_gate_up,
    think_down,
    talk_proj,
    codec_table,
    codec_ids,
    talk_gain,
    talk_routes,
    talk_weights,
    talk_keep,
    talk_gate_up,
    talk_down,
):
    steps = jnp.asarray(
        [[((a * 4 + c) * 4 + p) * 4 + q for a, c, p, q in order] for order in (THINK_ORDER, TALK_ORDER)], jnp.int32
    )
    wide = PARTNERS * SLOT
    hbm = pl.BlockSpec(memory_space=pltpu.HBM)
    small = (
        steps,
        tokens,
        think_gain.reshape(1, -1),
        think_routes.T,
        think_weights.T,
        think_keep.T,
        codec_ids.reshape(1, -1),
        talk_gain.reshape(1, -1),
        talk_routes.T,
        talk_weights.T,
        talk_keep.T,
    )
    large = (think_gate_up, think_down, codec_table, talk_proj, talk_gate_up, talk_down)
    outs = (
        jax.ShapeDtypeStruct(tokens.shape, BF16),
        jax.ShapeDtypeStruct((ROWS, talk_proj.shape[1]), BF16),
    )

    def exchange(halves, hidden_width):
        width = halves * 1024
        return [
            pltpu.VMEM((wide, halves * 128), BF16),
            pltpu.VMEM((wide, halves * 128), BF16),
            pltpu.VMEM((256, width), BF16),
            pltpu.VMEM((256, hidden_width), BF16),
            pltpu.VMEM((256, width), BF16),
            pltpu.VMEM((wide, halves * 128), BF16),
            pltpu.VMEM((wide, halves * 128), BF16),
        ]

    held = pl.pallas_call(
        step_kernel,
        out_shape=outs,
        in_specs=[hbm] * (len(small) + len(large)),
        out_specs=(hbm, hbm),
        scratch_shapes=[pltpu.VMEM(a.shape, a.dtype) for a in small + large + outs]
        + [pltpu.VMEM((rows, wide), BF16) for rows in (128, 256, 128, 256)]
        + exchange(2, think_down.shape[1])
        + exchange(1, talk_down.shape[1])
        + [
            pltpu.SemaphoreType.DMA((len(small),)),
            pltpu.SemaphoreType.DMA((len(large),)),
            pltpu.SemaphoreType.DMA((4,)),
            pltpu.SemaphoreType.DMA((2, max(len(THINK_CHUNKS), len(TALK_CHUNKS)))),
            pltpu.SemaphoreType.DMA((2,)),
            pltpu.SemaphoreType.DMA((2,)),
            pltpu.SemaphoreType.REGULAR,
        ],
        compiler_params=pltpu.CompilerParams(
            collective_id=0, has_side_effects=True, vmem_limit_bytes=56 * 2**20
        ),
        name="moe_step",
    )(*small, *large)
    return pl.pallas_call(hand_over, out_shape=outs, name="hand_over")(*held)


def solution(mesh):
    rows = P(AXES, None)
    experts = P(AXES, None, None)
    return jax.shard_map(
        shards,
        mesh=mesh,
        in_specs=(rows, P(), rows, rows, rows, experts, experts, P(), P(), P(AXES), P(), rows, rows, rows, experts, experts),
        out_specs=(rows, rows),
        check_vma=False,
    )
```

time: 79.2 us -> 66.4 us (0.84)
  local copies, waits for them, and re-layouts: 11 us -> 0 us
  Pallas kernels: 67.1 us -> 65.6 us
    unnamed x8 -> x0, local copies, waits for them, and re-layouts: 11 us -> none
    pallas_call x1 -> x2, Pallas kernels: 67.1 us -> 65.6 us  [the longest x1 64.1 us: shards(): pl.pallas_call(step_kernel, out_shape=outs, in_specs=[hbm] * (len(small)...]
where the time goes in v2:
time: 66.4 us; the launch traced here: 66.3 us
  Pallas kernels  65.6 us (99%)
    pallas_call x1, Pallas kernels, shards(): pl.pallas_call(step_kernel, out_shape=outs, in_specs=[hbm] * (len(small)...  64.1 us
    pallas_call x1, Pallas kernels, shards(): return pl.pallas_call(hand_over, out_shape=outs, name='hand_over')(*held)  1.48 us

profile of v2, /device:TPU:1, one launch (start us, length us, event | category | flops | bytes accessed | tf_op | source)
XLA Modules:
  0.0 66.3 jit_solution(1173565684363005866)
XLA Ops:
  0.6 64.1 %moe_step.1 = (bf16[16,2048]{1,0:T(8,128)(2,1)}, bf16[16,1024]{1,0:T(8,128)(2,1)}) custom-call(s32[2,128]{1,0:T(2,128)} %constant.2.clone.refs_0_, bf16[16,2048]{1,0:T(8,128)(2,1)} %refs_1_.1, f32[1,2048]{1,0:T(1,128)} %bitcast.9, s32[8,16]{1,0:T(8,128)} %bitcast.10, f32[8,16]{1,0:T(8,128)} %bitcast.11, s32[8,16]{1,0:T(8,128)} %bitcast.12, ...), custom_call_target="tpu_custom_call" | custom-call | tf_op jit(solution)/shard_map/moe_step/pallas_call | solution.py:368
  64.8 1.5 %hand_over.1 = (bf16[16,2048]{1,0:T(8,128)(2,1)}, bf16[16,1024]{1,0:T(8,128)(2,1)}) custom-call(bf16[16,2048]{1,0:T(8,128)(2,1)} %get-tuple-element.4.think_in, bf16[16,1024]{1,0:T(8,128)(2,1)} %get-tuple-element.5.talk_in), custom_call_target="tpu_custom_call" | custom-call | tf_op jit(solution)/shard_map/hand_over/pallas_call | solution.py:391

commit v3 on v2

--- a/solution.py
+++ b/solution.py
@@ -180,10 +180,14 @@
                         c * 32 : (c + 1) * 32, h * 128 : (h + 1) * 128
                     ]
         span = slice(first * 2, last * 2)
-        tile = 256 if hidden_width % 256 == 0 else 128
+        tile = 256 if hidden_width % 256 == 0 else hidden_width
         for n in range(hidden_width // tile):
-            gate = dot(rows[span, :], gate_up[0, :, n * tile : (n + 1) * tile])
-            up = dot(rows[span, :], gate_up[0, :, hidden_width + n * tile : hidden_width + (n + 1) * tile])
+            if tile == hidden_width:
+                both = dot(rows[span, :], gate_up[0])
+                gate, up = both[:, :tile], both[:, tile:]
+            else:
+                gate = dot(rows[span, :], gate_up[0, :, n * tile : (n + 1) * tile])
+                up = dot(rows[span, :], gate_up[0, :, hidden_width + n * tile : hidden_width + (n + 1) * tile])
             hidden[span, n * tile : (n + 1) * tile] = (gate / (1.0 + jnp.exp(-gate)) * up).astype(BF16)
         for n in range(width // 256):
             results[span, n * 256 : (n + 1) * 256] = dot(
@@ -224,8 +228,6 @@
 
     place = my_place()
     barrier = pltpu.get_barrier_semaphore()
-    for step in NEAR:
-        pl.semaphore_signal(barrier, inc=1, device_id=device_at(place, step, 1), device_id_type=MESH)
     smalls = [pltpu.make_async_copy(a, b, small_sem.at[i]) for i, (a, b) in enumerate(zip(small, here))]
     loads = [
         pltpu.make_async_copy(a, b, load_sem.at[i])
@@ -233,8 +235,10 @@
             zip((gate_up1, down1, table_hbm, proj_hbm, gate_up2, down2), (gu1, dn1, table, proj, gu2, dn2))
         )
     ]
-    for load in smalls + loads:
+    for load in smalls:
         load.start()
+    for step in NEAR:
+        pl.semaphore_signal(barrier, inc=1, device_id=device_at(place, step, 1), device_id_type=MESH)
     for load in smalls:
         load.wait()
 
@@ -251,6 +255,8 @@
     send(range(EARLY), THINK_CHUNKS, send_sem.at[0], there_recv.at[0])
     pl.semaphore_wait(relay_sem, len(RELAYS))
     send(range(EARLY, PARTNERS - 1), THINK_CHUNKS, send_sem.at[0], there_recv.at[0])
+    for load in loads:
+        load.start()
 
     route_tables(place, steps[1:2, :], routes2[...], weights2[...], keep2[...], pick2, mix2)
     loads[2].wait()

time: 66.4 us -> 61.9 us (0.932)
  Pallas kernels: 65.6 us -> 61.1 us
    pallas_call x1, Pallas kernels: 64.1 us -> 59.6 us  [shards(): pl.pallas_call(step_kernel, out_shape=outs, in_specs=[hbm] * (len(small)...]
where the time goes in v3:
time: 61.9 us; the launch traced here: 61.7 us
  Pallas kernels  61.1 us (99%)
  between operations  0.64 us (1%)
    pallas_call x1, Pallas kernels, shards(): pl.pallas_call(step_kernel, out_shape=outs, in_specs=[hbm] * (len(small)...  59.6 us
    pallas_call x1, Pallas kernels, shards(): return pl.pallas_call(hand_over, out_shape=outs, name='hand_over')(*held)  1.48 us

profile of v3, /device:TPU:1, one launch (start us, length us, event | category | flops | bytes accessed | tf_op | source)
XLA Modules:
  0.0 61.7 jit_solution(9311637193844443384)
XLA Ops:
  0.6 59.6 %moe_step.1 = (bf16[16,2048]{1,0:T(8,128)(2,1)}, bf16[16,1024]{1,0:T(8,128)(2,1)}) custom-call(s32[2,128]{1,0:T(2,128)} %constant.2.clone.refs_0_, bf16[16,2048]{1,0:T(8,128)(2,1)} %refs_1_.1, f32[1,2048]{1,0:T(1,128)} %bitcast.9, s32[8,16]{1,0:T(8,128)} %bitcast.10, f32[8,16]{1,0:T(8,128)} %bitcast.11, s32[8,16]{1,0:T(8,128)} %bitcast.12, ...), custom_call_target="tpu_custom_call" | custom-call | tf_op jit(solution)/shard_map/moe_step/pallas_call | solution.py:374
  60.3 1.5 %hand_over.1 = (bf16[16,2048]{1,0:T(8,128)(2,1)}, bf16[16,1024]{1,0:T(8,128)(2,1)}) custom-call(bf16[16,2048]{1,0:T(8,128)(2,1)} %get-tuple-element.4.think_in, bf16[16,1024]{1,0:T(8,128)(2,1)} %get-tuple-element.5.talk_in), custom_call_target="tpu_custom_call" | custom-call | tf_op jit(solution)/shard_map/hand_over/pallas_call | solution.py:397

commit v4 on v3

--- a/solution.py
+++ b/solution.py
@@ -32,7 +32,7 @@
 TALK_ORDER = partner_order((6, 5, 4, 3, 2, 1, 0))
 EARLY = sum(hops(step) == 3 for step in THINK_ORDER)
 THINK_CHUNKS = ((0, 48), (48, 128))
-TALK_CHUNKS = ((0, 48), (48, 128))
+TALK_CHUNKS = ((0, 32), (32, 128))
 NEAR = [step for step in THINK_ORDER[:-1] if hops(step) <= 3]
 RELAYS = ((0, 1, 1, 1), (0, 3, 3, 3))
 
@@ -96,9 +96,11 @@
     block = (lane >> 1) & 7
     for c in range(8):
         here = block == c
-        pick_ref[c * ROWS : (c + 1) * ROWS, :] = jnp.where(here, parts[0], 0.0).astype(BF16)
-        mix_ref[c * ROWS : (c + 1) * ROWS, :] = jnp.where(here, parts[1], 0.0).astype(BF16)
-        mix_ref[128 + c * ROWS : 128 + (c + 1) * ROWS, :] = jnp.where(here, parts[2], 0.0).astype(BF16)
+        if pick_ref is not None:
+            pick_ref[c * ROWS : (c + 1) * ROWS, :] = jnp.where(here, parts[0], 0.0).astype(BF16)
+        if mix_ref is not None:
+            mix_ref[c * ROWS : (c + 1) * ROWS, :] = jnp.where(here, parts[1], 0.0).astype(BF16)
+            mix_ref[128 + c * ROWS : 128 + (c + 1) * ROWS, :] = jnp.where(here, parts[2], 0.0).astype(BF16)
 
 
 def by_blocks(rows, halves):
@@ -159,7 +161,7 @@
     ).astype(BF16)
 
 
-def run_expert(place, order, chunks, halves, mix, gate_up, down, bufs, sems):
+def run_expert(idle, place, order, chunks, halves, mix, gate_up, down, bufs, sems):
     bins, arrived, rows, hidden, results, packed, returned = bufs
     there_recv, back_send, back_recv = sems
     width = halves * 1024
@@ -212,6 +214,7 @@
                 part = pl.ds(j * SLOT, SLOT)
                 copy_to(packed.at[part], returned.at[part], device_at(place, order[j], -1), back_send, back_recv).start()
     returned[own, :] = packed[own, :]
+    idle()
     wait_bytes(returned, 0, PARTNERS - 1, back_recv)
     total = dot(mix[...], returned[...])
     return unblock(total[:128] + total[128:], halves)
@@ -223,7 +226,7 @@
     here, (gu1, dn1, table, proj, gu2, dn2) = refs[19:30], refs[30:36]
     think_row, talk_row, pick1, mix1, pick2, mix2 = refs[36:42]
     think_bufs, talk_bufs = refs[42:49], refs[49:56]
-    small_sem, load_sem, send_sem, there_recv, back_recv, out_sem, relay_sem = refs[56:]
+    small_sem, load_sem, send_sem, there_recv, back_recv, out_sem, relay_sem, codec_row = refs[56:]
     steps, tokens, gain1, routes1, weights1, keep1, codec_ids, gain2, routes2, weights2, keep2 = here
 
     place = my_place()
@@ -241,9 +244,11 @@
         pl.semaphore_signal(barrier, inc=1, device_id=device_at(place, step, 1), device_id_type=MESH)
     for load in smalls:
         load.wait()
+    for load in loads[:2]:
+        load.start()
 
     normed = rms_rows(tokens[...].astype(F32), gain1[...])
-    route_tables(place, steps[0:1, :], routes1[...], weights1[...], keep1[...], pick1, mix1)
+    route_tables(place, steps[0:1, :], routes1[...], weights1[...], keep1[...], pick1, None)
     bins, arrived = think_bufs[:2]
     blocks = by_blocks(normed, 2)
     for g in range(8):
@@ -255,18 +260,23 @@
     send(range(EARLY), THINK_CHUNKS, send_sem.at[0], there_recv.at[0])
     pl.semaphore_wait(relay_sem, len(RELAYS))
     send(range(EARLY, PARTNERS - 1), THINK_CHUNKS, send_sem.at[0], there_recv.at[0])
-    for load in loads:
-        load.start()
-
+
+    route_tables(place, steps[0:1, :], routes1[...], weights1[...], keep1[...], None, mix1)
     route_tables(place, steps[1:2, :], routes2[...], weights2[...], keep2[...], pick2, mix2)
-    loads[2].wait()
-    vocab = table.shape[0]
-    ids = jnp.transpose(jnp.broadcast_to(codec_ids[...], (8, ROWS)))[:, :1]
-    chosen = jnp.where(iota((ROWS, vocab), 1) == ids, 1.0, 0.0).astype(BF16)
-    codec = dot(chosen, table[...])
+
+    def find_codec():
+        for load in loads[2:]:
+            load.start()
+        loads[2].wait()
+        vocab = table.shape[0]
+        ids = jnp.transpose(jnp.broadcast_to(codec_ids[...], (8, ROWS)))[:, :1]
+        chosen = jnp.where(iota((ROWS, vocab), 1) == ids, 1.0, 0.0).astype(BF16)
+        codec_row[...] = dot(chosen, table[...])
+
     loads[0].wait()
     loads[1].wait()
     mixed = run_expert(
+        find_codec,
         place,
         THINK_ORDER,
         THINK_CHUNKS,
@@ -283,7 +293,7 @@
     think_store.start()
 
     loads[3].wait()
-    talk_input = dot(think, proj[...]) + codec
+    talk_input = dot(think, proj[...]) + codec_row[...]
     blocks = by_blocks(rms_rows(talk_input, gain2[...]), 1)
     bins, arrived = talk_bufs[:2]
     for g in range(8):
@@ -293,6 +303,7 @@
     loads[4].wait()
     loads[5].wait()
     mixed = run_expert(
+        lambda: None,
         place,
         TALK_ORDER,
         TALK_CHUNKS,
@@ -388,6 +399,7 @@
             pltpu.SemaphoreType.DMA((2,)),
             pltpu.SemaphoreType.DMA((2,)),
             pltpu.SemaphoreType.REGULAR,
+            pltpu.VMEM((ROWS, talk_proj.shape[1]), F32),
         ],
         compiler_params=pltpu.CompilerParams(
             collective_id=0, has_side_effects=True, vmem_limit_bytes=56 * 2**20

time: 61.9 us -> 61.3 us (level)
    pallas_call x1, Pallas kernels: 59.6 us -> 59 us  [shards(): pl.pallas_call(step_kernel, out_shape=outs, in_specs=[hbm] * (len(small)...]
where the time goes in v4:
time: 61.3 us; the launch traced here: 61.1 us
  Pallas kernels  60.5 us (99%)
  between operations  0.64 us (1%)
    pallas_call x1, Pallas kernels, shards(): pl.pallas_call(step_kernel, out_shape=outs, in_specs=[hbm] * (len(small)...  59 us
    pallas_call x1, Pallas kernels, shards(): return pl.pallas_call(hand_over, out_shape=outs, name='hand_over')(*held)  1.48 us

profile of v4, /device:TPU:1, one launch (start us, length us, event | category | flops | bytes accessed | tf_op | source)
XLA Modules:
  0.0 61.1 jit_solution(6881731412186699055)
XLA Ops:
  0.6 59.0 %moe_step.1 = (bf16[16,2048]{1,0:T(8,128)(2,1)}, bf16[16,1024]{1,0:T(8,128)(2,1)}) custom-call(s32[2,128]{1,0:T(2,128)} %constant.2.clone.refs_0_, bf16[16,2048]{1,0:T(8,128)(2,1)} %refs_1_.1, f32[1,2048]{1,0:T(1,128)} %bitcast.9, s32[8,16]{1,0:T(8,128)} %bitcast.10, f32[8,16]{1,0:T(8,128)} %bitcast.11, s32[8,16]{1,0:T(8,128)} %bitcast.12, ...), custom_call_target="tpu_custom_call" | custom-call | tf_op jit(solution)/shard_map/moe_step/pallas_call | solution.py:385
  59.6 1.5 %hand_over.1 = (bf16[16,2048]{1,0:T(8,128)(2,1)}, bf16[16,1024]{1,0:T(8,128)(2,1)}) custom-call(bf16[16,2048]{1,0:T(8,128)(2,1)} %get-tuple-element.4.think_in, bf16[16,1024]{1,0:T(8,128)(2,1)} %get-tuple-element.5.talk_in), custom_call_target="tpu_custom_call" | custom-call | tf_op jit(solution)/shard_map/hand_over/pallas_call | solution.py:409
